TPU v7x, 32 devices: a whole 2x2x4 slice. The times are simulated.
32 devices in a mesh: seq: 8 (over y, x, core), head: 4 (over z).
Axes of the slice: x: 2, y: 2, z: 4, core: 2. Of those that a mesh axis runs over, the one named last changes fastest.
Arguments:
- activations: bfloat16 [4096, 5376], P(('seq', 'head')), may hold values from -42 to 42, as said below
- input_gain: float32 [5376], replicated, may hold values from 0.1 to 1.9
- query_weight: bfloat16 [5376, 4096], P(None, 'head'), may hold values from -2.2818633 to 2.2818633
- key_weight: bfloat16 [5376, 2048], P(None, 'head'), may hold values from -1 to 1
- value_weight: bfloat16 [5376, 2048], P(None, 'head'), may hold values from -0.078125 to 0.078125
- output_weight: bfloat16 [4096, 5376], P('head'), may hold values from -0.09375 to 0.09375
- cache_edge: bfloat16 [2, 1024, 2048], P(None, None, 'head'), may hold values from -6 to 6
- post_gain: float32 [5376], replicated, may hold values from 0.1 to 1.9
Outputs:
- layer_out: bfloat16 [4096, 5376], P(('seq', 'head'))
Inputs may be any that keep to these rules, and one draw needn't show every extreme that they name: `activations`: input rows with row and feature scales.
All inputs are finite; a program needn't handle non-finite values.
Results may differ from a plain program's by a relative error of at most 0.006.
Values may be sent and summed in bfloat16 or wider, within the bound.
A program may use at most 128 MiB of HBM per device.

v0:
```python
import jax
import jax.numpy as jnp
from jax import lax
from jax.sharding import PartitionSpec as P

HD = 128
WINDOW = 1024
SCALAR = 168
TOK_DEV = 512


EPSILON = 1e-06
ROPE_BASE = 10000.0


def from_behind(array, axis, by):
    count = lax.axis_size(axis)
    pairs = [(i, i + by) for i in range(count) if 0 <= i + by < count]
    return lax.ppermute(array, axis, pairs)


def normalize_rows(values, gain):
    return values * lax.rsqrt(jnp.mean(values * values, axis=-1, keepdims=True) + EPSILON) * gain


def rotate(vectors, positions):
    half_size = vectors.shape[-1] // 2
    frequency = ROPE_BASE ** (-(jnp.arange(half_size, dtype=jnp.float32) * 2.0 / vectors.shape[-1]))
    angles = positions[:, None] * frequency[None, :]
    cosine = jnp.cos(angles)[:, None, :]
    sine_part = jnp.sin(angles)[:, None, :]
    first_half = vectors[..., :half_size]
    second_half = vectors[..., half_size:]
    return jnp.concatenate(
        [
            first_half * cosine - second_half * sine_part,
            second_half * cosine + first_half * sine_part,
        ],
        axis=-1,
    )


def per_device(
    activations,
    input_gain,
    query_weight,
    key_weight,
    value_weight,
    output_weight,
    cache_edge,
    post_gain,
):
    heads_query = query_weight.shape[1] // HD
    heads_kv = key_weight.shape[1] // HD
    group_size = heads_query // heads_kv
    query_width = heads_query * HD
    kv_width = heads_kv * HD
    seq_pos = lax.axis_index("seq")
    first_pos = seq_pos * TOK_DEV
    normed = normalize_rows(
        lax.all_gather(activations, "head", axis=0, tiled=True).astype(jnp.float32), input_gain
    ).astype(jnp.bfloat16)
    row_count = normed.shape[0]
    positions = (first_pos + jnp.arange(row_count, dtype=jnp.int32)).astype(jnp.float32)
    queries_raw = jnp.dot(normed, query_weight, preferred_element_type=jnp.float32)
    keys_raw = jnp.dot(normed, key_weight, preferred_element_type=jnp.float32)
    value_rows = jnp.dot(normed, value_weight, preferred_element_type=jnp.float32)
    queries = rotate(queries_raw.reshape(row_count, heads_query, HD), positions) * SCALAR ** (-0.5)
    keys = rotate(keys_raw.reshape(row_count, heads_kv, HD), positions)
    joined = jnp.concatenate(
        [queries.reshape(row_count, query_width), keys.reshape(row_count, kv_width), value_rows],
        axis=1,
    )
    packed = joined.astype(jnp.bfloat16)
    queries = packed[:, :query_width]
    own_edge = packed[:, query_width:]
    cache_rows = jnp.concatenate([cache_edge[0], cache_edge[1]], axis=1)
    reach_steps = WINDOW // TOK_DEV
    earlier = []
    received = own_edge
    for distance in range(1, reach_steps + 1):
        received = from_behind(own_edge, "seq", distance)
        offset = jnp.clip(WINDOW + (seq_pos - distance) * TOK_DEV, 0, WINDOW - TOK_DEV)
        from_cache = lax.dynamic_slice_in_dim(cache_rows, offset, TOK_DEV, 0)
        earlier.append(jnp.where(seq_pos >= distance, received, from_cache))
    window_rows = jnp.concatenate(earlier[::-1] + [own_edge], axis=0)
    span_length = window_rows.shape[0]
    key_rows = window_rows[:, :kv_width].reshape(span_length, heads_kv, HD)
    value_block = window_rows[:, kv_width:].reshape(span_length, heads_kv, HD)
    query_block = queries.reshape(TOK_DEV, heads_kv, group_size, HD)
    query_index = jnp.arange(TOK_DEV, dtype=jnp.int32)
    key_index = jnp.arange(span_length, dtype=jnp.int32)
    allowed = (key_index[None, :] > query_index[:, None]) & (
        key_index[None, :] <= query_index[:, None] + WINDOW
    )
    scores = jnp.einsum("qgrd,kgd->grqk", query_block, key_rows, preferred_element_type=jnp.float32)
    scores = jnp.where(allowed[None, None], scores, -jnp.inf)
    largest = jnp.max(scores, axis=-1, keepdims=True)
    exps = jnp.exp(scores - largest)
    probabilities = (exps / jnp.sum(exps, axis=-1, keepdims=True)).astype(jnp.bfloat16)
    attended = jnp.einsum(
        "grqk,kgd->qgrd", probabilities, value_block, preferred_element_type=jnp.float32
    )
    attended = attended.astype(jnp.bfloat16).reshape(TOK_DEV, query_width)
    projected = lax.psum_scatter(
        jnp.dot(attended, output_weight, preferred_element_type=jnp.float32),
        "head",
        scatter_dimension=0,
        tiled=True,
    )
    branch = normalize_rows(projected, post_gain)
    return (activations.astype(jnp.float32) + branch).astype(jnp.bfloat16)


def solution(mesh):
    return jax.shard_map(
        per_device,
        mesh=mesh,
        in_specs=(
            P(("seq", "head"), None),
            P(),
            P(None, "head"),
            P(None, "head"),
            P(None, "head"),
            P("head", None),
            P(None, None, "head"),
            P(),
        ),
        out_specs=P(("seq", "head"), None),
        check_vma=False,
    )
```

profile of v0, /device:TPU:21, one launch (start us, length us, event | category | flops | bytes accessed | tf_op | source)
XLA Modules:
  0.0 423.2 jit_solution(8933734952359513674)
XLA Ops:
  7.9 0.8 copy.11
  8.7 0.8 copy.12
  9.6 1.7 fusion.25
  12.4 1.4 fusion.10
  13.8 96.9 %all-gather.2.cloned.1.call-done = bf16[512,5376]{1,0:T(8,128)(2,1)} async-done(((bf16[128,5376]{1,0:T(8,128)(2,1)}), bf16[512,5376]{1,0:T(8,128)(2,1)}) %all-gather.2.cloned.1.call-update) | async-done | bytes 5505040 | tf_op jit(solution)/shard_map/all_gather | solution.py:61
  110.7 3.9 fusion.5
  114.9 6.0 %fusion.22 = f32[512,512]{0,1:T(8,128)S(1)} fusion(bf16[5376,512]{1,0:T(8,128)(2,1)} %param.11, bf16[512,5376]{1,0:T(8,128)(2,1)S(1)} %copy-done, f32[5376]{0:T(1024)S(1)} %copy-done.5, f32[512]{0:T(512)S(1)} %add_rsqrt_fusion), kind=kOutput, calls=%fused_computation.48 | convolution fusion | flops 2829582336 | bytes 12082176 | tf_op jit(solution)/shard_map/dot_general | solution.py:66
  121.2 3.4 convolution_convert_fusion
  124.7 3.8 collective-permute-start.1
  128.5 2.1 collective-permute-start
  130.6 8.7 %convolution_bitcast_fusion = f32[64,8,8,128]{3,1,2,0:T(8,128)S(1)} fusion(bf16[5376,1024]{1,0:T(8,128)(2,1)} %param.10, bf16[512,5376]{1,0:T(8,128)(2,1)S(1)} %copy-done, f32[5376]{0:T(1024)S(1)} %copy-done.5, f32[512]{0:T(512)S(1)} %add_rsqrt_fusion), kind=kOutput, calls=%fused_computation.28 | convolution fusion | flops 5648154624 | bytes 18635776 | tf_op jit(solution)/shard_map/dot_general | solution.py:65
  139.8 1.1 multiply_subtract_fusion
  141.6 7.2 %collective-permute-done.1 = bf16[512,1024]{0,1:T(8,128)(2,1)S(1)} collective-permute-done((bf16[512,1024]{0,1:T(8,128)(2,1)S(1)}, bf16[512,1024]{0,1:T(8,128)(2,1)S(1)}, u32[]{:S(2)}, u32[]{:S(2)}) %collective-permute-start.1) | collective-permute-done | bytes 1048608 | tf_op jit(solution)/shard_map/ppermute | solution.py:19
  148.9 15.4 %collective-permute-done = bf16[512,1024]{0,1:T(8,128)(2,1)S(1)} collective-permute-done((bf16[512,1024]{0,1:T(8,128)(2,1)S(1)}, bf16[512,1024]{0,1:T(8,128)(2,1)S(1)}, u32[]{:S(2)}, u32[]{:S(2)}) %collective-permute-start) | collective-permute-done | bytes 1048608 | tf_op jit(solution)/shard_map/ppermute | solution.py:19
  164.3 2.2 fusion.16
  166.5 9.5 %maximum_maximum_fusion = bf16[1536,1024]{0,1:T(8,128)(2,1)S(1)} fusion(bf16[512,512]{0,1:T(8,128)(2,1)S(1)} %convolution_convert_fusion, bf16[512,512]{0,1:T(8,128)(2,1)S(1)} %bitcast.48, bf16[512,1024]{0,1:T(8,128)(2,1)S(1)} %get-tuple-element.10, bf16[512,1024]{0,1:T(8,128)(2,1)S(1)} %get-tuple-element.9), kind=kLoop, calls=%fused_computation.14 | loop fusion | flops 12582912 | bytes 6291456 | tf_op jit(solution)/shard_map/concatenate | solution.py:86
  176.0 1.4 fusion.24
  177.5 11.8 %fusion.27 = f32[4,1536,512,2]{2,1,3,0:T(8,128)} fusion(bf16[1536,4,128,1]{0,2,3,1:T(8,128)(2,1)S(1)} %bitcast.45, bf16[512,4,2,128]{3,0,2,1:T(8,128)(2,1)S(1)} %bitcast.51), kind=kOutput, calls=%fused_computation.52 | convolution fusion | flops 1610612736 | bytes 27787264 | tf_op jit(solution)/shard_map/qgrd,kgd->grqk/dot_general | solution.py:96
  189.2 9.0 %fusion.26 = f32[4,2,512]{2,1,0:T(2,128)S(1)} fusion(pred[512,1536]{0,1:T(8,128)(4,1)} %fusion.10, bf16[1536,4,128,1]{0,2,3,1:T(8,128)(2,1)S(1)} %bitcast.46, bf16[512,4,2,128]{3,0,2,1:T(8,128)(2,1)S(1)} %bitcast.52), kind=kOutput, calls=%fused_computation.51 | convolution fusion | flops 1629488640 | bytes 3424256 | tf_op jit(solution)/shard_map/sub | solution.py:99
  198.3 13.0 %fusion.12 = bf16[4,128,2,512]{3,1,2,0:T(8,128)(2,1)S(1)} fusion(bf16[1536,4,128,1]{0,2,3,1:T(8,128)(2,1)} %bitcast.53, f32[4,2,512]{2,1,0:T(2,128)S(1)} %fusion.26, f32[4,1536,512,2]{2,1,3,0:T(8,128)} %fusion.27, pred[512,1536]{0,1:T(8,128)(4,1)} %fusion.10), kind=kOutput, calls=%fused_computation.29 | convolution fusion | flops 1636308480 | bytes 28590080 | tf_op jit(solution)/shard_map/grqk,kgd->qgrd/dot_general | solution.py:101
  211.2 13.0 %fusion.28 = f32[512,5376]{1,0:T(8,128)} fusion(bf16[512,1024]{0,1:T(8,128)(2,1)S(1)} %bitcast.54, bf16[1024,5376]{1,0:T(8,128)(2,1)} %param.13), kind=kOutput, calls=%fused_computation.53 | convolution fusion | flops 5637144576 | bytes 23068672 | tf_op jit(solution)/shard_map/dot_general | solution.py:106
  224.3 186.3 %reduce-scatter.2.cloned.1.call-done = f32[128,5376]{1,0:T(8,128)} async-done(((f32[512,5376]{1,0:T(8,128)}), f32[128,5376]{1,0:T(8,128)}) %reduce-scatter.2.cloned.1.call-update) | async-done | bytes 2752528 | tf_op jit(solution)/shard_map/reduce_scatter | solution.py:105
  410.6 2.1 multiply_reduce_fusion
  412.6 3.3 add_convert_fusion
  (35 shorter events, 4.2 us)
Async XLA Ops:
  6.5 104.1 %all-gather.2.cloned.1.call-start = ((), (), s32[]{:S(2)}) async-start(), calls=%async_computation.1 | async-start | bytes 6881280 | tf_op jit(solution)/shard_map/all_gather | solution.py:61
  7.3 403.3 %reduce-scatter.2.cloned.1.call-start = ((), (), s32[]{:S(2)}) async-start(), calls=%async_computation.2 | async-start | bytes 13762560 | tf_op jit(solution)/shard_map/reduce_scatter | solution.py:105
  11.2 103.3 %copy-start.5 = (f32[5376]{0:T(1024)S(1)}, f32[5376]{0:T(1024)}, u32[]{:S(2)}) copy-start(f32[5376]{0:T(1024)} %param.9) | copy-start | bytes 64516
  110.7 4.2 copy-start
  110.7 10.5 %slice-start = ((s8[5505024]{0:T(1024)(128)(4,1)}), s8[4194304]{0:T(1024)(128)(4,1)S(1)}, s32[]{:S(2)}) async-start(s8[5505024]{0:T(1024)(128)(4,1)} %bitcast.56), calls=%async_computation.3 | async-start | bytes 8388608
  114.9 6.3 %slice-start.1 = ((s8[5505024]{0:T(1024)(128)(4,1)}), s8[1310720]{0:T(1024)(128)(4,1)S(1)}, s32[]{:S(2)}) async-start(s8[5505024]{0:T(1024)(128)(4,1)} %bitcast.56), calls=%async_computation.4 | async-start | bytes 2621440
  124.6 15.1 %copy-start.2 = (f32[512,64]{1,0:T(8,128)S(1)}, f32[512,64]{1,0:T(8,128)}, u32[]{:S(2)}) copy-start(f32[512,64]{1,0:T(8,128)} %copy.11) | copy-start | bytes 393220
  124.7 15.1 %copy-start.3 = (f32[512,64]{1,0:T(8,128)S(1)}, f32[512,64]{1,0:T(8,128)}, u32[]{:S(2)}) copy-start(f32[512,64]{1,0:T(8,128)} %copy.12) | copy-start | bytes 393220
  124.7 24.2 %collective-permute-start.1 = (bf16[512,1024]{0,1:T(8,128)(2,1)S(1)}, bf16[512,1024]{0,1:T(8,128)(2,1)S(1)}, u32[]{:S(2)}, u32[]{:S(2)}) collective-permute-start(bf16[512,1024]{0,1:T(8,128)(2,1)S(1)} %pad_maximum_fusion), channel_id=1, source_target_pairs={{0,4},{4,8},{8,12},{12,16},{16,20},{20,24},{24,28},{1,5},{5,9},{9,... | collective-permute-start | bytes 3145736 | tf_op jit(solution)/shard_map/ppermute | solution.py:19
  128.5 35.8 %collective-permute-start = (bf16[512,1024]{0,1:T(8,128)(2,1)S(1)}, bf16[512,1024]{0,1:T(8,128)(2,1)S(1)}, u32[]{:S(2)}, u32[]{:S(2)}) collective-permute-start(bf16[512,1024]{0,1:T(8,128)(2,1)S(1)} %pad_maximum_fusion), channel_id=1, source_target_pairs={{0,8},{4,12},{8,16},{12,20},{16,24},{20,28},{1,9},{5,13},{9,17},{1... | collective-permute-start | bytes 3145736 | tf_op jit(solution)/shard_map/ppermute | solution.py:19
  224.2 188.4 %copy-start.1 = (bf16[128,5376]{1,0:T(8,128)(2,1)S(1)}, bf16[128,5376]{1,0:T(8,128)(2,1)}, u32[]{:S(2)}) copy-start(bf16[128,5376]{1,0:T(8,128)(2,1)} %param.8) | copy-start | bytes 4128772
  224.2 188.4 %copy-start.4 = (f32[5376]{0:T(1024)S(1)}, f32[5376]{0:T(1024)}, u32[]{:S(2)}) copy-start(f32[5376]{0:T(1024)} %param.15) | copy-start | bytes 64516
Sparse Core Ops, SparseCore 0:
  8.9 101.7 all-gather.1
  224.4 186.1 reduce-scatter.1
where the time goes:
time: 431 us; the launch traced here: 423 us
  waiting for transfers between devices  307 us (71%)
  matrix products  64.9 us (15%)
  other arithmetic  24.9 us (6%)
  between operations  14.1 us (3%)
  local copies, waits for them, and re-layouts  6.78 us (2%)
  starting transfers between devices  5.96 us (1%)
    reduce_scatter x1, waiting for transfers between devices, per_device(): lax.psum_scatter(jnp.dot(attended, output_weight, preferred_element_type=...  186 us
    all_gather x1, waiting for transfers between devices, per_device(): lax.all_gather(activations, 'head', axis=0, tiled=True).astype(jnp.float32)  96.9 us
    ppermute x2, waiting for transfers between devices, from_behind(): return lax.ppermute(array, axis, pairs)  22.7 us
    dot_general x1, matrix products, per_device(): jnp.dot(attended, output_weight, preferred_element_type=jnp.float32)  13 us
    dot_general x1, matrix products, per_device(): jnp.einsum('grqk,kgd->qgrd', probabilities, value_block, preferred_elemen...  13 us
    dot_general x1, matrix products, per_device(): jnp.einsum('qgrd,kgd->grqk', query_block, key_rows, preferred_element_typ...  11.8 us
    concatenate x1, other arithmetic, per_device(): window_rows = jnp.concatenate(earlier[::-1] + [own_edge], axis=0)  9.52 us
    sub x1, matrix products, per_device(): exps = jnp.exp(scores - largest)  9.03 us
  transfers between devices with their start and end apart: 4, of which 4 were waited for; matrix products, arithmetic and copies ran while one was open for 4% of the time, Pallas kernels for 0%

commit v1 on v0

--- a/solution.py
+++ b/solution.py
@@ -57,9 +57,8 @@
     kv_width = heads_kv * HD
     seq_pos = lax.axis_index("seq")
     first_pos = seq_pos * TOK_DEV
-    normed = normalize_rows(
-        lax.all_gather(activations, "head", axis=0, tiled=True).astype(jnp.float32), input_gain
-    ).astype(jnp.bfloat16)
+    normed = normalize_rows(activations.astype(jnp.float32), input_gain).astype(jnp.bfloat16)
+    normed = lax.all_gather(normed, "head", axis=0, tiled=True)
     row_count = normed.shape[0]
     positions = (first_pos + jnp.arange(row_count, dtype=jnp.int32)).astype(jnp.float32)
     queries_raw = jnp.dot(normed, query_weight, preferred_element_type=jnp.float32)
@@ -103,11 +102,11 @@
     )
     attended = attended.astype(jnp.bfloat16).reshape(TOK_DEV, query_width)
     projected = lax.psum_scatter(
-        jnp.dot(attended, output_weight, preferred_element_type=jnp.float32),
+        jnp.dot(attended, output_weight, preferred_element_type=jnp.float32).astype(jnp.bfloat16),
         "head",
         scatter_dimension=0,
         tiled=True,
-    )
+    ).astype(jnp.float32)
     branch = normalize_rows(projected, post_gain)
     return (activations.astype(jnp.float32) + branch).astype(jnp.bfloat16)
 

time: 431 us -> 341 us (0.79)
  the two profiles are of different devices: /device:TPU:21 before, /device:TPU:0 now
where the time goes in v1:
time: 341 us; the launch traced here: 335 us
  waiting for transfers between devices  219 us (64%)
  matrix products  64.8 us (19%)
  other arithmetic  24.9 us (7%)
  between operations  14.1 us (4%)
  local copies, waits for them, and re-layouts  7 us (2%)
  starting transfers between devices  5.59 us (2%)
    reduce_scatter x1, waiting for transfers between devices, per_device(): lax.psum_scatter(jnp.dot(attended, output_weight, preferred_element_type=...  106 us
    all_gather x1, waiting for transfers between devices, per_device(): normed = lax.all_gather(normed, 'head', axis=0, tiled=True)  98.7 us
    ppermute x2, waiting for transfers between devices, from_behind(): return lax.ppermute(array, axis, pairs)  14.6 us
    dot_general x1, matrix products, per_device(): jnp.einsum('grqk,kgd->qgrd', probabilities, value_block, preferred_elemen...  13 us
    dot_general x1, matrix products, per_device(): jnp.dot(attended, output_weight, preferred_element_type=jnp.float32)  11.9 us
    dot_general x1, matrix products, per_device(): jnp.einsum('qgrd,kgd->grqk', query_block, key_rows, preferred_element_typ...  11.8 us
    concatenate x1, other arithmetic, per_device(): window_rows = jnp.concatenate(earlier[::-1] + [own_edge], axis=0)  9.53 us
    sub x1, matrix products, per_device(): exps = jnp.exp(scores - largest)  9.26 us
  transfers between devices with their start and end apart: 4, of which 3 were waited for; matrix products, arithmetic and copies ran while one was open for 4% of the time, Pallas kernels for 0%

profile of v1, /device:TPU:0, one launch (start us, length us, event | category | flops | bytes accessed | tf_op | source)
XLA Modules:
  0.0 335.3 jit_solution(6270335785261173082)
XLA Ops:
  6.5 1.7 fusion.10
  8.2 2.8 fusion.12
  11.7 0.8 copy.11
  12.5 0.8 copy.12
  13.4 1.7 fusion.24
  16.1 1.5 fusion.7
  17.6 98.7 %all-gather.2.cloned.1.call-done = bf16[512,5376]{1,0:T(8,128)(2,1)} async-done(((bf16[128,5376]{1,0:T(8,128)(2,1)}), bf16[512,5376]{1,0:T(8,128)(2,1)}) %all-gather.2.cloned.1.call-update) | async-done | bytes 5505040 | tf_op jit(solution)/shard_map/all_gather | solution.py:61
  116.3 7.3 %fusion.26 = f32[512,512]{0,1:T(8,128)S(1)} fusion(bf16[512,5376]{1,0:T(8,128)(2,1)} %all-gather.2.cloned.1.call-done, bf16[5376,512]{1,0:T(8,128)(2,1)} %param.11), kind=kOutput, calls=%fused_computation.56 | convolution fusion | flops 2818572288 | bytes 12058624 | tf_op jit(solution)/shard_map/dot_general | solution.py:65
  123.9 5.8 %convolution_convert_fusion.1 = bf16[512,512]{0,1:T(8,128)(2,1)S(1)} fusion(bf16[512,5376]{1,0:T(8,128)(2,1)S(1)} %copy-done.4, bf16[5376,512]{1,0:T(8,128)(2,1)} %param.12), kind=kOutput, calls=%fused_computation.35 | convolution fusion | flops 2818834432 | bytes 11534336 | tf_op jit(solution)/shard_map/dot_general | solution.py:66
  129.8 2.0 collective-permute-start.1
  131.8 3.5 %collective-permute-start = (bf16[512,1024]{0,1:T(8,128)(2,1)S(1)}, bf16[512,1024]{0,1:T(8,128)(2,1)S(1)}, u32[]{:S(2)}, u32[]{:S(2)}) collective-permute-start(bf16[512,1024]{0,1:T(8,128)(2,1)S(1)} %pad_maximum_fusion), channel_id=1, source_target_pairs={{0,8},{4,12},{8,16},{12,20},{16,24},{20,28},{1,9},{5,13},{9,17},{1... | collective-permute-start | bytes 3145736 | tf_op jit(solution)/shard_map/ppermute | solution.py:19
  135.4 5.8 %convolution_bitcast_fusion = f32[64,8,8,128]{3,1,2,0:T(8,128)S(1)} fusion(bf16[512,5376]{1,0:T(8,128)(2,1)S(1)} %copy-done.4, bf16[5376,1024]{1,0:T(8,128)(2,1)S(1)} %bitcast.59), kind=kOutput, calls=%fused_computation.33 | convolution fusion | flops 5637144576 | bytes 18612224 | tf_op jit(solution)/shard_map/dot_general | solution.py:64
  142.2 1.1 multiply_subtract_fusion
  144.1 14.6 %collective-permute-done = bf16[512,1024]{0,1:T(8,128)(2,1)S(1)} collective-permute-done((bf16[512,1024]{0,1:T(8,128)(2,1)S(1)}, bf16[512,1024]{0,1:T(8,128)(2,1)S(1)}, u32[]{:S(2)}, u32[]{:S(2)}) %collective-permute-start) | collective-permute-done | bytes 1048608 | tf_op jit(solution)/shard_map/ppermute | solution.py:19
  158.7 2.2 fusion.19
  160.9 9.5 %maximum_maximum_fusion = bf16[1536,1024]{0,1:T(8,128)(2,1)S(1)} fusion(bf16[512,512]{0,1:T(8,128)(2,1)S(1)} %convolution_convert_fusion.1, bf16[512,512]{0,1:T(8,128)(2,1)S(1)} %bitcast.51, bf16[512,1024]{0,1:T(8,128)(2,1)S(1)} %get-tuple-element.10, bf16[512,1024]{0,1:T(8,128)(2,1)S(1)} %get-tuple-element.9), kind=kLoop, calls=%fused_computation.15 | loop fusion | flops 12582912 | bytes 6291456 | tf_op jit(solution)/shard_map/concatenate | solution.py:85
  170.4 1.4 fusion.23
  171.8 11.8 %fusion.27 = f32[4,1536,512,2]{2,1,3,0:T(8,128)} fusion(bf16[1536,4,128,1]{0,2,3,1:T(8,128)(2,1)S(1)} %bitcast.48, bf16[512,4,2,128]{3,0,2,1:T(8,128)(2,1)S(1)} %bitcast.54), kind=kOutput, calls=%fused_computation.57 | convolution fusion | flops 1610612736 | bytes 27787264 | tf_op jit(solution)/shard_map/qgrd,kgd->grqk/dot_general | solution.py:95
  183.6 9.3 %fusion.25 = f32[4,2,512]{2,1,0:T(2,128)S(1)} fusion(pred[512,1536]{0,1:T(8,128)(4,1)} %fusion.7, bf16[1536,4,128,1]{0,2,3,1:T(8,128)(2,1)S(1)} %bitcast.49, bf16[512,4,2,128]{3,0,2,1:T(8,128)(2,1)S(1)} %bitcast.55), kind=kOutput, calls=%fused_computation.55 | convolution fusion | flops 1629488640 | bytes 3424256 | tf_op jit(solution)/shard_map/sub | solution.py:98
  192.9 13.0 %fusion.15 = bf16[4,128,2,512]{3,1,2,0:T(8,128)(2,1)S(1)} fusion(bf16[1536,4,128,1]{0,2,3,1:T(8,128)(2,1)} %bitcast.56, f32[4,2,512]{2,1,0:T(2,128)S(1)} %fusion.25, f32[4,1536,512,2]{2,1,3,0:T(8,128)} %fusion.27, pred[512,1536]{0,1:T(8,128)(4,1)} %fusion.7), kind=kOutput, calls=%fused_computation.34 | convolution fusion | flops 1636308480 | bytes 28590080 | tf_op jit(solution)/shard_map/grqk,kgd->qgrd/dot_general | solution.py:100
  205.8 11.9 %convolution_convert_fusion = bf16[512,5376]{1,0:T(8,128)(2,1)} fusion(bf16[512,1024]{0,1:T(8,128)(2,1)S(1)} %bitcast.60, bf16[1024,5376]{1,0:T(8,128)(2,1)} %param.13), kind=kOutput, calls=%fused_computation.8 | convolution fusion | flops 5639897088 | bytes 17563648 | tf_op jit(solution)/shard_map/dot_general | solution.py:105
  217.7 105.6 %reduce-scatter.2.cloned.1.call-done = bf16[128,5376]{1,0:T(8,128)(2,1)} async-done(((bf16[512,5376]{1,0:T(8,128)(2,1)}), bf16[128,5376]{1,0:T(8,128)(2,1)}) %reduce-scatter.2.cloned.1.call-update) | async-done | bytes 1376272 | tf_op jit(solution)/shard_map/reduce_scatter | solution.py:104
  323.4 1.7 fusion.8
  325.1 3.0 fusion.13
  (36 shorter events, 3.8 us)
Async XLA Ops:
  6.5 109.8 %all-gather.2.cloned.1.call-start = ((), (), s32[]{:S(2)}) async-start(), calls=%async_computation.1 | async-start | bytes 6881280 | tf_op jit(solution)/shard_map/all_gather | solution.py:61
  11.1 312.3 %reduce-scatter.2.cloned.1.call-start = ((), (), s32[]{:S(2)}) async-start(), calls=%async_computation.2 | async-start | bytes 6881280 | tf_op jit(solution)/shard_map/reduce_scatter | solution.py:104
  116.3 7.6 %copy-start.4 = (bf16[512,5376]{1,0:T(8,128)(2,1)S(1)}, bf16[512,5376]{1,0:T(8,128)(2,1)}, u32[]{:S(2)}) copy-start(bf16[512,5376]{1,0:T(8,128)(2,1)} %all-gather.2.cloned.1.call-done) | copy-start | bytes 16515076
  123.8 11.5 %slice-start = ((s8[11010048]{0:T(1024)(128)(4,1)}), s8[4194304]{0:T(1024)(128)(4,1)S(1)}, s32[]{:S(2)}) async-start(s8[11010048]{0:T(1024)(128)(4,1)} %bitcast.58), calls=%async_computation.3 | async-start | bytes 8388608
  123.9 11.5 %slice-start.1 = ((s8[11010048]{0:T(1024)(128)(4,1)}), s8[4194304]{0:T(1024)(128)(4,1)S(1)}, s32[]{:S(2)}) async-start(s8[11010048]{0:T(1024)(128)(4,1)} %bitcast.58), calls=%async_computation.4 | async-start | bytes 8388608
  123.9 11.4 %slice-start.2 = ((s8[11010048]{0:T(1024)(128)(4,1)}), s8[2621440]{0:T(1024)(128)(4,1)S(1)}, s32[]{:S(2)}) async-start(s8[11010048]{0:T(1024)(128)(4,1)} %bitcast.58), calls=%async_computation.5 | async-start | bytes 5242880
  129.8 14.3 %collective-permute-start.1 = (bf16[512,1024]{0,1:T(8,128)(2,1)S(1)}, bf16[512,1024]{0,1:T(8,128)(2,1)S(1)}, u32[]{:S(2)}, u32[]{:S(2)}) collective-permute-start(bf16[512,1024]{0,1:T(8,128)(2,1)S(1)} %pad_maximum_fusion), channel_id=1, source_target_pairs={{0,4},{4,8},{8,12},{12,16},{16,20},{20,24},{24,28},{1,5},{5,9},{9,... | collective-permute-start | bytes 3145736 | tf_op jit(solution)/shard_map/ppermute | solution.py:19
  131.8 26.9 %collective-permute-start = (bf16[512,1024]{0,1:T(8,128)(2,1)S(1)}, bf16[512,1024]{0,1:T(8,128)(2,1)S(1)}, u32[]{:S(2)}, u32[]{:S(2)}) collective-permute-start(bf16[512,1024]{0,1:T(8,128)(2,1)S(1)} %pad_maximum_fusion), channel_id=1, source_target_pairs={{0,8},{4,12},{8,16},{12,20},{16,24},{20,28},{1,9},{5,13},{9,17},{1... | collective-permute-start | bytes 3145736 | tf_op jit(solution)/shard_map/ppermute | solution.py:19
  141.2 1.0 copy-start.1
  141.2 1.0 copy-start.2
  217.7 107.4 %copy-start = (bf16[128,5376]{1,0:T(8,128)(2,1)S(1)}, bf16[128,5376]{1,0:T(8,128)(2,1)}, u32[]{:S(2)}) copy-start(bf16[128,5376]{1,0:T(8,128)(2,1)} %param.8) | copy-start | bytes 4128772
  217.7 107.4 %copy-start.3 = (f32[5376]{0:T(1024)S(1)}, f32[5376]{0:T(1024)}, u32[]{:S(2)}) copy-start(f32[5376]{0:T(1024)} %param.15) | copy-start | bytes 64516
Sparse Core Ops, SparseCore 0:
  11.2 105.0 all-gather.1
  217.9 105.4 reduce-scatter.1

commit v2 on v1

v2 whole, which is shorter than its diff:
```python
import functools
import jax
import jax.numpy as jnp
from jax import lax
from jax.experimental import pallas as pl
from jax.experimental.pallas import tpu as pltpu
from jax.sharding import PartitionSpec as P

HD = 128
WINDOW = 1024
SCALAR = 168
TOK_DEV = 512
EPSILON = 1e-06
ROPE_BASE = 10000.0
REACH = WINDOW // TOK_DEV
ROW_CHUNKS = 2
COL_CHUNKS = 3
MESH = pl.DeviceIdType.MESH


def rope_tables(positions):
    half_size = HD // 2
    frequency = ROPE_BASE ** (-(jnp.arange(half_size, dtype=jnp.float32) * 2.0 / HD))
    angles = positions[:, None] * frequency[None, :]
    cosine = jnp.cos(angles)
    sine = jnp.sin(angles)
    return jnp.concatenate([cosine, cosine], axis=1), jnp.concatenate([-sine, sine], axis=1)


def kernel(
    n, s_count,
    act_ref, gain_ref, wq_hbm, wk_hbm, wv_hbm, wo_hbm, cache_hbm, post_ref, cos_ref, sin_ref,
    out_ref,
    wq, wk, wv, wo, rows, q_buf, kv, att, slots, acc,
    w_sem, cache_sem, ag_send, ag_recv, kv_send, kv_recv, rs_send, rs_recv,
):
    s = lax.axis_index("seq")
    z = lax.axis_index("head")
    R, D = act_ref.shape
    kv_width = wk.shape[1]
    heads_kv = kv_width // HD
    group = wq.shape[1] // kv_width
    CR = R // ROW_CHUNKS
    CD = D // COL_CHUNKS

    weight_copies = [
        pltpu.make_async_copy(src, dst, w_sem.at[i])
        for i, (src, dst) in enumerate([(wq_hbm, wq), (wk_hbm, wk), (wv_hbm, wv), (wo_hbm, wo)])
    ]
    for c in weight_copies:
        c.start()

    def cache_copies(d):
        return [
            pltpu.make_async_copy(
                cache_hbm.at[i, pl.ds(pl.multiple_of(WINDOW + (s - d) * TOK_DEV, TOK_DEV), TOK_DEV), :],
                kv.at[pl.ds(WINDOW - d * TOK_DEV, TOK_DEV), pl.ds(i * kv_width, kv_width)],
                cache_sem.at[d - 1, i],
            )
            for i in range(2)
        ]

    for d in range(1, REACH + 1):
        @pl.when(s < d)
        def _():
            for c in cache_copies(d):
                c.start()

    barrier = pltpu.get_barrier_semaphore()

    def greet(cond, ds, dz):
        @pl.when(cond)
        def _():
            pl.semaphore_signal(barrier, inc=1, device_id=(s + ds, z + dz), device_id_type=MESH)

    partners = [(z > 0, 0, -1), (z < n - 1, 0, 1)]
    for d in range(1, REACH + 1):
        partners += [(s >= d, -d, 0), (s + d < s_count, d, 0)]
    for p in partners:
        greet(*p)

    def norm_chunk(i, carry):
        r0 = pl.multiple_of(i * 16, 16)
        x = act_ref[pl.ds(r0, 16), :].astype(jnp.float32)
        y = x * lax.rsqrt(jnp.mean(x * x, axis=-1, keepdims=True) + EPSILON) * gain_ref[...]
        rows[z, pl.ds(r0, 16), :] = y.astype(jnp.bfloat16)
        return carry

    lax.fori_loop(0, R // 16, norm_chunk, 0)
    pl.semaphore_wait(barrier, sum(jnp.where(p[0], 1, 0) for p in partners))

    right = lax.rem(z + 1, n)
    left = lax.rem(z + n - 1, n)

    def ag_copy(direction, block, c):
        where = rows.at[block, pl.ds(c * CR, CR), :]
        return pltpu.make_async_remote_copy(
            src_ref=where, dst_ref=where,
            send_sem=ag_send.at[direction, block, c], recv_sem=ag_recv.at[direction, block, c],
            device_id=(s, right if direction == 0 else left), device_id_type=MESH,
        )

    def kv_copy(d, block):
        r0 = pl.multiple_of(block * R, R)
        return pltpu.make_async_remote_copy(
            src_ref=kv.at[pl.ds(WINDOW + r0, R), :],
            dst_ref=kv.at[pl.ds(WINDOW - d * TOK_DEV + r0, R), :],
            send_sem=kv_send.at[d - 1, block], recv_sem=kv_recv.at[d - 1, block],
            device_id=(lax.rem(s + d, s_count), z), device_id_type=MESH,
        )

    def rs_copy(direction, block, slot, c):
        where = slots.at[slot, c]
        return pltpu.make_async_remote_copy(
            src_ref=where, dst_ref=where,
            send_sem=rs_send.at[direction, block, c], recv_sem=rs_recv.at[direction, block, c],
            device_id=(s, right if direction == 0 else left), device_id_type=MESH,
        )

    def project(block):
        r0 = pl.multiple_of(block * R, R)
        cosine = cos_ref[pl.ds(r0, R), :]
        sine = sin_ref[pl.ds(r0, R), :]

        def run(w, tile, rotary, scale, dst, dst_r0, dst_c0):
            def one(i, carry):
                c0 = pl.multiple_of(i * tile, tile)
                t = jnp.dot(rows[block], w[:, pl.ds(c0, tile)], preferred_element_type=jnp.float32)
                for h in range(tile // HD):
                    u = t[:, h * HD:(h + 1) * HD]
                    if rotary:
                        u = u * cosine + pltpu.roll(u, HD // 2, 1) * sine
                    if scale is not None:
                        u = u * scale
                    dst[pl.ds(dst_r0, R), pl.ds(pl.multiple_of(dst_c0 + c0 + h * HD, HD), HD)] = u.astype(jnp.bfloat16)
                return carry
            lax.fori_loop(0, w.shape[1] // tile, one, 0)

        tile = min(256, kv_width)
        own = pl.multiple_of(WINDOW + r0, R)
        run(wk, tile, True, None, kv, own, 0)
        run(wv, tile, False, None, kv, own, kv_width)
        for d in range(1, REACH + 1):
            @pl.when(s + d < s_count)
            def _():
                kv_copy(d, block).start()
        run(wq, 256, True, SCALAR ** (-0.5), q_buf, r0, 0)

    def first_sends(direction, cond):
        @pl.when(cond)
        def _():
            for c in range(ROW_CHUNKS):
                ag_copy(direction, z, c).start()

    first_sends(0, z < n - 1)
    first_sends(1, z > 0)
    for i in (1, 2, 0):
        weight_copies[i].wait()
    project(z)

    def gather_step(t, carry):
        from_left = z - t
        from_right = z + t
        for c in range(ROW_CHUNKS):
            @pl.when(from_left >= 0)
            def _():
                ag_copy(0, from_left, c).wait_recv()

                @pl.when(z < n - 1)
                def _():
                    ag_copy(0, from_left, c).start()

            @pl.when(from_right < n)
            def _():
                ag_copy(1, from_right, c).wait_recv()

                @pl.when(z > 0)
                def _():
                    ag_copy(1, from_right, c).start()

        @pl.when(from_left >= 0)
        def _():
            project(from_left)

        @pl.when(from_right < n)
        def _():
            project(from_right)
        return carry

    lax.fori_loop(1, n, gather_step, 0)

    for d in range(1, REACH + 1):
        @pl.when(s < d)
        def _():
            for c in cache_copies(d):
                c.wait()

        @pl.when(s >= d)
        def _():
            lax.fori_loop(0, n, lambda b, carry: (kv_copy(d, b).wait_recv(), carry)[1], 0)
    weight_copies[3].wait()

    row_i = lax.broadcasted_iota(jnp.int32, (group * R, R), 0)
    row_i = lax.rem(row_i, R)
    col_i = lax.broadcasted_iota(jnp.int32, (group * R, R), 1)
    later = col_i > row_i
    spans = [(0, R), (R, WINDOW - R), (WINDOW, R)]

    def attend(block):
        r0 = pl.multiple_of(block * R, R)
        for g in range(heads_kv):
            q = jnp.concatenate(
                [q_buf[pl.ds(r0, R), (g * group + a) * HD:(g * group + a + 1) * HD] for a in range(group)], axis=0
            )
            scores = []
            for j, (o, w) in enumerate(spans):
                k = kv[pl.ds(pl.multiple_of(r0 + o, R), w), g * HD:(g + 1) * HD]
                sc = lax.dot_general(q, k, (((1,), (1,)), ((), ())), preferred_element_type=jnp.float32)
                if j == 0:
                    sc = jnp.where(later, sc, -jnp.inf)
                if j == 2:
                    sc = jnp.where(later, -jnp.inf, sc)
                scores.append(sc)
            m = functools.reduce(jnp.maximum, [jnp.max(x, axis=-1, keepdims=True) for x in scores])
            total = 0.0
            o_sum = 0.0
            for (o, w), sc in zip(spans, scores):
                e = jnp.exp(sc - m)
                total = total + jnp.sum(e, axis=-1, keepdims=True)
                v = kv[pl.ds(pl.multiple_of(r0 + o, R), w), kv_width + g * HD:kv_width + (g + 1) * HD]
                o_sum = o_sum + jnp.dot(e.astype(jnp.bfloat16), v, preferred_element_type=jnp.float32)
            o_sum = (o_sum / total).astype(jnp.bfloat16)
            for a in range(group):
                att[:, (g * group + a) * HD:(g * group + a + 1) * HD] = o_sum[a * R:(a + 1) * R]

    TILE = 256

    def partial_out(direction, block, incoming):
        attend(block)
        for c in range(COL_CHUNKS):
            @pl.when(incoming)
            def _():
                rs_copy(direction, block, block, c).wait_recv()

            def one(i, carry):
                c0 = pl.multiple_of(i * TILE, TILE)
                w0 = pl.multiple_of(c * CD + i * TILE, TILE)
                p = jnp.dot(att[...], wo[:, pl.ds(w0, TILE)], preferred_element_type=jnp.float32)
                before = slots[block, c, :, pl.ds(c0, TILE)].astype(jnp.float32)
                p = p + jnp.where(incoming, before, 0.0)
                slots[block, c, :, pl.ds(c0, TILE)] = p.astype(jnp.bfloat16)
                return carry
            lax.fori_loop(0, CD // TILE, one, 0)
            send_out(direction, block, c).start()

    def send_out(direction, block, c):
        if direction == 0:
            return rs_copy(0, block, block, c)
        last = jnp.where(block == z - 1, n, block)
        return pltpu.make_async_remote_copy(
            src_ref=slots.at[block, c], dst_ref=slots.at[last, c],
            send_sem=rs_send.at[1, block, c], recv_sem=rs_recv.at[1, block, c],
            device_id=(s, left), device_id_type=MESH,
        )

    def scatter_step(t, carry):
        to_right = n - t
        to_left = t - 1

        @pl.when(to_right > z)
        def _():
            partial_out(0, to_right, z > 0)

        @pl.when(to_left < z)
        def _():
            partial_out(1, to_left, z < n - 1)
        return carry

    lax.fori_loop(1, n, scatter_step, 0)

    attend(z)

    def own(i, carry):
        w0 = pl.multiple_of(i * TILE, TILE)
        acc[:, pl.ds(w0, TILE)] = jnp.dot(att[...], wo[:, pl.ds(w0, TILE)], preferred_element_type=jnp.float32)
        return carry
    lax.fori_loop(0, D // TILE, own, 0)

    for c in range(COL_CHUNKS):
        for direction, slot, cond in ((0, z, z > 0), (1, n, z < n - 1)):
            @pl.when(cond)
            def _():
                rs_copy(direction, z, slot, c).wait_recv()
                acc[:, c * CD:(c + 1) * CD] += slots[slot, c].astype(jnp.float32)

    def finish(i, carry):
        r0 = pl.multiple_of(i * 16, 16)
        x = acc[pl.ds(r0, 16), :]
        y = x * lax.rsqrt(jnp.mean(x * x, axis=-1, keepdims=True) + EPSILON) * post_ref[...]
        out_ref[pl.ds(r0, 16), :] = (act_ref[pl.ds(r0, 16), :].astype(jnp.float32) + y).astype(jnp.bfloat16)
        return carry
    lax.fori_loop(0, R // 16, finish, 0)

    def drain(b, carry):
        @pl.when((b <= z) & (z < n - 1))
        def _():
            for c in range(ROW_CHUNKS):
                ag_copy(0, b, c).wait_send()

        @pl.when((b >= z) & (z > 0))
        def _():
            for c in range(ROW_CHUNKS):
                ag_copy(1, b, c).wait_send()

        @pl.when(b > z)
        def _():
            for c in range(COL_CHUNKS):
                send_out(0, b, c).wait_send()

        @pl.when(b < z)
        def _():
            for c in range(COL_CHUNKS):
                send_out(1, b, c).wait_send()

        for d in range(1, REACH + 1):
            @pl.when(s + d < s_count)
            def _():
                kv_copy(d, b).wait_send()
        return carry
    lax.fori_loop(0, n, drain, 0)


def per_device(n, s_count, act, gain, wq, wk, wv, wo, cache, post):
    R, D = act.shape
    s = lax.axis_index("seq")
    positions = (s * TOK_DEV + jnp.arange(TOK_DEV, dtype=jnp.int32)).astype(jnp.float32)
    cosine, sine = rope_tables(positions)
    bf, f32 = jnp.bfloat16, jnp.float32
    vmem = pl.BlockSpec(memory_space=pltpu.VMEM)
    hbm = pl.BlockSpec(memory_space=pl.ANY)
    dma = pltpu.SemaphoreType.DMA
    return pl.pallas_call(
        functools.partial(kernel, n, s_count),
        out_shape=jax.ShapeDtypeStruct((R, D), bf),
        in_specs=[vmem, vmem, hbm, hbm, hbm, hbm, hbm, vmem, vmem, vmem],
        out_specs=vmem,
        scratch_shapes=[
            pltpu.VMEM(wq.shape, bf),
            pltpu.VMEM(wk.shape, bf),
            pltpu.VMEM(wv.shape, bf),
            pltpu.VMEM(wo.shape, bf),
            pltpu.VMEM((n, R, D), bf),
            pltpu.VMEM((TOK_DEV, wq.shape[1]), bf),
            pltpu.VMEM((WINDOW + TOK_DEV, 2 * wk.shape[1]), bf),
            pltpu.VMEM((R, wo.shape[0]), bf),
            pltpu.VMEM((n + 1, COL_CHUNKS, R, D // COL_CHUNKS), bf),
            pltpu.VMEM((R, D), f32),
            dma((4,)),
            dma((REACH, 2)),
            dma((2, n, ROW_CHUNKS)),
            dma((2, n, ROW_CHUNKS)),
            dma((REACH, n)),
            dma((REACH, n)),
            dma((2, n, COL_CHUNKS)),
            dma((2, n, COL_CHUNKS)),
        ],
        compiler_params=pltpu.CompilerParams(
            collective_id=0, has_side_effects=True, vmem_limit_bytes=62 * 1024 * 1024
        ),
    )(act, gain.reshape(1, -1), wq, wk, wv, wo, cache, post.reshape(1, -1), cosine, sine)


def solution(mesh):
    return jax.shard_map(
        functools.partial(per_device, mesh.shape["head"], mesh.shape["seq"]),
        mesh=mesh,
        in_specs=(
            P(("seq", "head"), None),
            P(),
            P(None, "head"),
            P(None, "head"),
            P(None, "head"),
            P("head", None),
            P(None, None, "head"),
            P(),
        ),
        out_specs=P(("seq", "head"), None),
        check_vma=False,
    )
```

time: 341 us -> 239 us (0.70)
  the two profiles are of different devices: /device:TPU:0 before, /device:TPU:21 now
where the time goes in v2:
time: 239 us
  Pallas kernels  232 us (97%)
  local copies, waits for them, and re-layouts  5.21 us (2%)
    pallas_call x1, Pallas kernels, per_device(): pl.pallas_call(functools.partial(kernel, n, s_count), out_shape=jax.Shape...  232 us

profile of v2, /device:TPU:21, one launch (start us, length us, event | category | flops | bytes accessed | tf_op | source)
XLA Modules:
  0.0 239.1 jit_solution(10801944004615372331)
XLA Ops:
  0.0 1.4 reshape.17.gain_ref
  1.4 1.3 reshape.18.post_ref
  2.7 1.0 fusion
  3.7 1.0 pad_maximum_fusion
  4.7 231.8 %shard_map.82 = bf16[128,5376]{1,0:T(8,128)(2,1)} custom-call(bf16[128,5376]{1,0:T(8,128)(2,1)} %act_ref.1, f32[1,5376]{1,0:T(1,128)} %reshape.17.gain_ref, bf16[5376,1024]{1,0:T(8,128)(2,1)} %wq_hbm.1, bf16[5376,512]{1,0:T(8,128)(2,1)} %wk_hbm.1, bf16[5376,512]{1,0:T(8,128)(2,1)} %wv_hbm.1, bf16[1024,5376]{1,0:T(8,128)(2,1)} %wo_hbm.1, ...), custom_call_target="tpu_custom_call" | custom-call | tf_op jit(solution)/shard_map/pallas_call | solution.py:342
  236.6 2.5 %copy.10 = bf16[128,5376]{1,0:T(8,128)(2,1)} copy(bf16[128,5376]{1,0:T(8,128)(2,1)} %shard_map.82) | data formatting | bytes 2752512
  (2 shorter events, 0.0 us)

commit v3 on v2

--- a/solution.py
+++ b/solution.py
@@ -13,7 +13,6 @@
 EPSILON = 1e-06
 ROPE_BASE = 10000.0
 REACH = WINDOW // TOK_DEV
-ROW_CHUNKS = 2
 COL_CHUNKS = 3
 MESH = pl.DeviceIdType.MESH
 
@@ -40,7 +39,8 @@
     kv_width = wk.shape[1]
     heads_kv = kv_width // HD
     group = wq.shape[1] // kv_width
-    CR = R // ROW_CHUNKS
+    row_chunks = ag_send.shape[2]
+    CR = R // row_chunks
     CD = D // COL_CHUNKS
 
     weight_copies = [
@@ -82,7 +82,7 @@
     def norm_chunk(i, carry):
         r0 = pl.multiple_of(i * 16, 16)
         x = act_ref[pl.ds(r0, 16), :].astype(jnp.float32)
-        y = x * lax.rsqrt(jnp.mean(x * x, axis=-1, keepdims=True) + EPSILON) * gain_ref[...]
+        y = x * lax.rsqrt(jnp.mean(x * x, axis=-1, keepdims=True) + EPSILON) * gain_ref[...].reshape(1, D)
         rows[z, pl.ds(r0, 16), :] = y.astype(jnp.bfloat16)
         return carry
 
@@ -149,19 +149,17 @@
     def first_sends(direction, cond):
         @pl.when(cond)
         def _():
-            for c in range(ROW_CHUNKS):
+            for c in range(row_chunks):
                 ag_copy(direction, z, c).start()
 
     first_sends(0, z < n - 1)
     first_sends(1, z > 0)
     for i in (1, 2, 0):
         weight_copies[i].wait()
-    project(z)
-
     def gather_step(t, carry):
         from_left = z - t
         from_right = z + t
-        for c in range(ROW_CHUNKS):
+        for c in range(row_chunks):
             @pl.when(from_left >= 0)
             def _():
                 ag_copy(0, from_left, c).wait_recv()
@@ -178,16 +176,21 @@
                 def _():
                     ag_copy(1, from_right, c).start()
 
+            if c == 0:
+                @pl.when(from_right - 1 < n)
+                def _():
+                    project(from_right - 1)
+
         @pl.when(from_left >= 0)
         def _():
             project(from_left)
-
-        @pl.when(from_right < n)
-        def _():
-            project(from_right)
         return carry
 
     lax.fori_loop(1, n, gather_step, 0)
+
+    @pl.when(z == 0)
+    def _():
+        project(n - 1)
 
     for d in range(1, REACH + 1):
         @pl.when(s < d)
@@ -296,7 +299,7 @@
     def finish(i, carry):
         r0 = pl.multiple_of(i * 16, 16)
         x = acc[pl.ds(r0, 16), :]
-        y = x * lax.rsqrt(jnp.mean(x * x, axis=-1, keepdims=True) + EPSILON) * post_ref[...]
+        y = x * lax.rsqrt(jnp.mean(x * x, axis=-1, keepdims=True) + EPSILON) * post_ref[...].reshape(1, D)
         out_ref[pl.ds(r0, 16), :] = (act_ref[pl.ds(r0, 16), :].astype(jnp.float32) + y).astype(jnp.bfloat16)
         return carry
     lax.fori_loop(0, R // 16, finish, 0)
@@ -304,12 +307,12 @@
     def drain(b, carry):
         @pl.when((b <= z) & (z < n - 1))
         def _():
-            for c in range(ROW_CHUNKS):
+            for c in range(row_chunks):
                 ag_copy(0, b, c).wait_send()
 
         @pl.when((b >= z) & (z > 0))
         def _():
-            for c in range(ROW_CHUNKS):
+            for c in range(row_chunks):
                 ag_copy(1, b, c).wait_send()
 
         @pl.when(b > z)
@@ -332,6 +335,7 @@
 
 def per_device(n, s_count, act, gain, wq, wk, wv, wo, cache, post):
     R, D = act.shape
+    row_chunks = min(2, R // 16)
     s = lax.axis_index("seq")
     positions = (s * TOK_DEV + jnp.arange(TOK_DEV, dtype=jnp.int32)).astype(jnp.float32)
     cosine, sine = rope_tables(positions)
@@ -357,8 +361,8 @@
             pltpu.VMEM((R, D), f32),
             dma((4,)),
             dma((REACH, 2)),
-            dma((2, n, ROW_CHUNKS)),
-            dma((2, n, ROW_CHUNKS)),
+            dma((2, n, row_chunks)),
+            dma((2, n, row_chunks)),
             dma((REACH, n)),
             dma((REACH, n)),
             dma((2, n, COL_CHUNKS)),
@@ -367,7 +371,7 @@
         compiler_params=pltpu.CompilerParams(
             collective_id=0, has_side_effects=True, vmem_limit_bytes=62 * 1024 * 1024
         ),
-    )(act, gain.reshape(1, -1), wq, wk, wv, wo, cache, post.reshape(1, -1), cosine, sine)
+    )(act, gain, wq, wk, wv, wo, cache, post, cosine, sine)
 
 
 def solution(mesh):

time: 239 us -> 237 us (level)
  local copies, waits for them, and re-layouts: 5.21 us -> 2.51 us
    reshape x2 -> x0, local copies, waits for them, and re-layouts: 2.7 us -> none  [the longest x1 1.36 us: per_device(): gain.reshape(1, -1)]
where the time goes in v3:
time: 237 us; the launch traced here: 236 us
  Pallas kernels  232 us (98%)
  local copies, waits for them, and re-layouts  2.51 us (1%)
    pallas_call x1, Pallas kernels, per_device(): pl.pallas_call(functools.partial(kernel, n, s_count), out_shape=jax.Shape...  232 us

profile of v3, /device:TPU:21, one launch (start us, length us, event | category | flops | bytes accessed | tf_op | source)
XLA Modules:
  0.0 236.3 jit_solution(12020655161048517489)
XLA Ops:
  0.0 1.0 fusion
  1.0 1.0 pad_maximum_fusion
  2.0 231.8 %shard_map.82 = bf16[128,5376]{1,0:T(8,128)(2,1)} custom-call(bf16[128,5376]{1,0:T(8,128)(2,1)} %act_ref.1, f32[5376]{0:T(1024)} %gain_ref.1, bf16[5376,1024]{1,0:T(8,128)(2,1)} %wq_hbm.1, bf16[5376,512]{1,0:T(8,128)(2,1)} %wk_hbm.1, bf16[5376,512]{1,0:T(8,128)(2,1)} %wv_hbm.1, bf16[1024,5376]{1,0:T(8,128)(2,1)} %wo_hbm.1, bf16[2,1024,512]{2,1,0:T(8,128)(2,1)} %cache_hbm.1, ...), custom_call_target="tpu_custom_call" | custom-call | tf_op jit(solution)/shard_map/pallas_call | solution.py:346
  233.8 2.5 %copy.10 = bf16[128,5376]{1,0:T(8,128)(2,1)} copy(bf16[128,5376]{1,0:T(8,128)(2,1)} %shard_map.82) | data formatting | bytes 2752512
  (2 shorter events, 0.0 us)

commit v4 on v3

--- a/solution.py
+++ b/solution.py
@@ -13,7 +13,7 @@
 EPSILON = 1e-06
 ROPE_BASE = 10000.0
 REACH = WINDOW // TOK_DEV
-COL_CHUNKS = 3
+COL_CHUNKS = 7
 MESH = pl.DeviceIdType.MESH
 
 
@@ -45,7 +45,7 @@
 
     weight_copies = [
         pltpu.make_async_copy(src, dst, w_sem.at[i])
-        for i, (src, dst) in enumerate([(wq_hbm, wq), (wk_hbm, wk), (wv_hbm, wv), (wo_hbm, wo)])
+        for i, (src, dst) in enumerate([(wk_hbm, wk), (wv_hbm, wv), (wq_hbm, wq), (wo_hbm, wo)])
     ]
     for c in weight_copies:
         c.start()
@@ -86,7 +86,6 @@
         rows[z, pl.ds(r0, 16), :] = y.astype(jnp.bfloat16)
         return carry
 
-    lax.fori_loop(0, R // 16, norm_chunk, 0)
     pl.semaphore_wait(barrier, sum(jnp.where(p[0], 1, 0) for p in partners))
 
     right = lax.rem(z + 1, n)
@@ -146,15 +145,18 @@
                 kv_copy(d, block).start()
         run(wq, 256, True, SCALAR ** (-0.5), q_buf, r0, 0)
 
-    def first_sends(direction, cond):
-        @pl.when(cond)
-        def _():
-            for c in range(row_chunks):
-                ag_copy(direction, z, c).start()
-
-    first_sends(0, z < n - 1)
-    first_sends(1, z > 0)
-    for i in (1, 2, 0):
+    for c in range(row_chunks):
+        lax.fori_loop(c * CR // 16, (c + 1) * CR // 16, norm_chunk, 0)
+
+        @pl.when(z < n - 1)
+        def _():
+            ag_copy(0, z, c).start()
+
+        @pl.when(z > 0)
+        def _():
+            ag_copy(1, z, c).start()
+
+    for i in range(3):
         weight_copies[i].wait()
     def gather_step(t, carry):
         from_left = z - t
@@ -335,7 +337,7 @@
 
 def per_device(n, s_count, act, gain, wq, wk, wv, wo, cache, post):
     R, D = act.shape
-    row_chunks = min(2, R // 16)
+    row_chunks = min(4, R // 16)
     s = lax.axis_index("seq")
     positions = (s * TOK_DEV + jnp.arange(TOK_DEV, dtype=jnp.int32)).astype(jnp.float32)
     cosine, sine = rope_tables(positions)

time: 237 us -> 226 us (0.954)
  Pallas kernels: 232 us -> 221 us
    pallas_call x1, Pallas kernels: 232 us -> 221 us  [per_device(): pl.pallas_call(functools.partial(kernel, n, s_count), out_shape=jax.Shape...]
where the time goes in v4:
time: 226 us
  Pallas kernels  221 us (98%)
  local copies, waits for them, and re-layouts  2.51 us (1%)
    pallas_call x1, Pallas kernels, per_device(): pl.pallas_call(functools.partial(kernel, n, s_count), out_shape=jax.Shape...  221 us

profile of v4, /device:TPU:21, one launch (start us, length us, event | category | flops | bytes accessed | tf_op | source)
XLA Modules:
  0.0 226.0 jit_solution(9304072331442685138)
XLA Ops:
  0.0 1.0 fusion
  1.0 1.0 pad_maximum_fusion
  2.0 221.4 %shard_map.82 = bf16[128,5376]{1,0:T(8,128)(2,1)} custom-call(bf16[128,5376]{1,0:T(8,128)(2,1)} %act_ref.1, f32[5376]{0:T(1024)} %gain_ref.1, bf16[5376,1024]{1,0:T(8,128)(2,1)} %wq_hbm.1, bf16[5376,512]{1,0:T(8,128)(2,1)} %wk_hbm.1, bf16[5376,512]{1,0:T(8,128)(2,1)} %wv_hbm.1, bf16[1024,5376]{1,0:T(8,128)(2,1)} %wo_hbm.1, bf16[2,1024,512]{2,1,0:T(8,128)(2,1)} %cache_hbm.1, ...), custom_call_target="tpu_custom_call" | custom-call | tf_op jit(solution)/shard_map/pallas_call | solution.py:348
  223.5 2.5 %copy.10 = bf16[128,5376]{1,0:T(8,128)(2,1)} copy(bf16[128,5376]{1,0:T(8,128)(2,1)} %shard_map.82) | data formatting | bytes 2752512
  (2 shorter events, 0.0 us)
